TPU v7x, 32 devices: a whole 2x2x4 slice. The times are simulated.
32 devices in a mesh: hist: 4 (over y, x), mom: 8 (over z, core).
Axes of the slice: x: 2, y: 2, z: 4, core: 2. Of those that a mesh axis runs over, the one named last changes fastest.
Arguments:
- statistic_now: float32 [256, 1024], P('mom', 'hist'), may hold values from -1.25 to 6.25
- statistic_prev: float32 [256, 1024], P('mom', 'hist'), may hold values from -2 to 7
- spectral_now: float32 [256, 1024], P('mom', 'hist'), may hold values from -1.5 to 1.5
- spectral_prev: float32 [256, 1024], P('mom', 'hist'), may hold values from -1.65 to 1.65
- statistic_hist: bfloat16 [1024, 256, 1024], P('hist', 'mom'), may hold values from -1.5 to 1.5
- spectral_hist: bfloat16 [1024, 256, 1024], P('hist', 'mom'), may hold values from -1.5 to 1.5
Outputs:
- statistic_end: float32 [256, 1024], P('mom', 'hist')
- spectral_end: float32 [256, 1024], P('mom', 'hist')
- memory_stat: float32 [256, 1024], P('mom', 'hist')
- memory_spec: float32 [256, 1024], P('mom', 'hist')
All inputs are finite; a program needn't handle non-finite values.
Results may differ from a plain program's by a relative error of at most 0.0029.
Values may be sent and summed in bfloat16 or wider, within the bound.
A program may use at most 128 MiB of HBM per device.

v0:
```python
import functools

import jax
import jax.numpy as jnp
import numpy as np
from jax import lax
from jax.experimental import pallas as pl
from jax.experimental.pallas import tpu as pltpu
from jax.sharding import PartitionSpec as P

STEPS = 2


time_step = 0.2
bare_mass = 0.04
cubic_coupling = 1.0 / 6.0
tadpole_coupling = 2.0
highest = lax.Precision.HIGHEST


def broadcast(block, axis, source):
    block = jnp.where(lax.axis_index(axis) == source, block, jnp.zeros_like(block))
    return lax.psum(block, axis)


def sine_table(mode_total):
    ordinal = jnp.arange(mode_total, dtype=jnp.float32) + 1.0
    return jnp.sqrt(2.0 / (mode_total + 1.0)) * jnp.sin(
        jnp.pi * ordinal[:, None] * ordinal[None, :] / (mode_total + 1.0)
    )


def omega_squared(mode_total, offset, amount):
    ordinal = (offset + jnp.arange(amount)).astype(jnp.float32) + 1.0
    return bare_mass + 4.0 * jnp.sin(jnp.pi * ordinal / (2.0 * (mode_total + 1.0))) ** 2


def self_energy(pos_stat, pos_spec):
    square_stat = pos_stat * pos_stat
    square_spec = pos_spec * pos_spec
    return (
        -cubic_coupling * pos_stat * (square_stat - 0.75 * square_spec),
        -cubic_coupling * pos_spec * (3.0 * square_stat - 0.25 * square_spec),
    )


def contract(weights, history):
    return jnp.einsum("ps,spu->pu", weights, history, preferred_element_type=jnp.float32)


def plain_device(
    statistic_now, statistic_prev, spectral_now, spectral_prev, statistic_hist, spectral_hist
):
    mode_count, time_count = statistic_now.shape
    hist_size = lax.axis_size("hist")
    mom_size = lax.axis_size("mom")
    hist_pos = lax.axis_index("hist")
    mom_pos = lax.axis_index("mom")
    mode_total = mode_count * mom_size
    window = statistic_hist.shape[2]
    sine_rows = sine_table(mode_total)
    frequency = omega_squared(mode_total, mom_pos * mode_count, mode_count)[:, None]
    zero_hist = jnp.zeros((), spectral_hist.dtype)
    times_own = hist_pos * time_count + jnp.arange(time_count)
    times_all = jnp.arange(window)
    lower_mask = times_own[:, None] <= times_all[None, :]
    upper_mask = times_own[:, None] >= times_all[None, :]
    spectral_low = jnp.where(lower_mask[:, None, :], spectral_hist, zero_hist)
    spectral_up = jnp.where(upper_mask[:, None, :], spectral_hist, zero_hist)
    stat_row, stat_old = (statistic_now, statistic_prev)
    spec_row, spec_old = (spectral_now, spectral_prev)
    memory_stat = jnp.zeros_like(statistic_now)
    memory_spec = jnp.zeros_like(spectral_now)
    for step_index in range(STEPS):
        partial_value = lax.psum(jnp.sum(stat_row[:, -1]), "mom")
        edge_total = broadcast(partial_value, "hist", hist_size - 1)
        tadpole = tadpole_coupling * edge_total / mode_total
        padded_stat = stat_row
        padded_spec = spec_row
        gather_stat, gather_spec = (
            lax.all_to_all(padded_stat, "mom", split_axis=1, concat_axis=0, tiled=True),
            lax.all_to_all(padded_spec, "mom", split_axis=1, concat_axis=0, tiled=True),
        )
        pos_stat = jnp.dot(
            sine_rows, gather_stat, precision=highest, preferred_element_type=jnp.float32
        )
        pos_spec = jnp.dot(
            sine_rows, gather_spec, precision=highest, preferred_element_type=jnp.float32
        )
        self_stat_pos, self_spec_pos = self_energy(pos_stat, pos_spec)
        back_stat = jnp.dot(
            sine_rows, self_stat_pos, precision=highest, preferred_element_type=jnp.float32
        ).astype(jnp.bfloat16)
        back_spec = jnp.dot(
            sine_rows, self_spec_pos, precision=highest, preferred_element_type=jnp.float32
        ).astype(jnp.bfloat16)
        modes_stat, modes_spec = (
            lax.all_to_all(back_stat, "mom", split_axis=0, concat_axis=1, tiled=True),
            lax.all_to_all(back_spec, "mom", split_axis=0, concat_axis=1, tiled=True),
        )
        part_stat = contract(modes_spec, statistic_hist) - contract(modes_stat, spectral_low)
        part_spec = contract(modes_spec, spectral_up)
        sum_stat, sum_spec = (
            lax.psum_scatter(part_stat, "hist", scatter_dimension=1, tiled=True),
            lax.psum_scatter(part_spec, "hist", scatter_dimension=1, tiled=True),
        )
        memory_stat = time_step * sum_stat
        memory_spec = time_step * sum_spec
        new_stat = (
            2.0 * stat_row
            - stat_old
            - time_step * time_step * ((frequency + tadpole) * stat_row + memory_stat)
        )
        new_spec = (
            2.0 * spec_row
            - spec_old
            - time_step * time_step * ((frequency + tadpole) * spec_row + memory_spec)
        )
        stat_old, stat_row = (stat_row, new_stat)
        spec_old, spec_row = (spec_row, new_spec)
    return (stat_row, spec_row, memory_stat, memory_spec)


LANES = 128
ROWS = 16
MESH = pl.DeviceIdType.MESH


def copy_to(axis, target, source, landing, send_sem, recv_sem):
    return pltpu.make_async_remote_copy(
        src_ref=source,
        dst_ref=landing,
        send_sem=send_sem,
        recv_sem=recv_sem,
        device_id={axis: target},
        device_id_type=MESH,
    )


def fused_kernel(
    hist_size,
    mom_size,
    stat_now_ref,
    stat_prev_ref,
    spec_now_ref,
    spec_prev_ref,
    stat_hist_ref,
    spec_hist_ref,
    forward_ref,
    back_ref,
    frequency_ref,
    stat_end_ref,
    spec_end_ref,
    memory_stat_ref,
    memory_spec_ref,
    stat_held,
    spec_held,
    low_mask,
    up_mask,
    spread,
    weights,
    row_send,
    row_recv,
    self_send,
    self_recv,
    part_send,
    part_recv,
    edge_send,
    edge_recv,
    hist_sem,
    row_sem,
    self_sem,
    part_sem,
    edge_sem,
):
    mode_count, time_count = stat_now_ref.shape
    half = mode_count // 2
    piece = time_count // mom_size
    depth = piece * mode_count
    mode_total = mode_count * mom_size
    here = lax.axis_index("hist")
    me = lax.axis_index("mom")
    order = [*range(1, hist_size), 0]

    loads = {}
    for turn in order:
        column = pl.multiple_of(lax.rem(here + turn, hist_size) * time_count, time_count)
        for which, (whole, held) in enumerate(
            ((stat_hist_ref, stat_held), (spec_hist_ref, spec_held))
        ):
            loads[turn, which] = pltpu.make_async_copy(
                whole.at[:, pl.ds(column, time_count)], held.at[turn], hist_sem.at[which, turn]
            )
            loads[turn, which].start()

    barrier = pltpu.get_barrier_semaphore()
    for offset in range(1, mom_size):
        pl.semaphore_signal(
            barrier, 1, device_id={"mom": lax.rem(me + offset, mom_size)}, device_id_type=MESH
        )
    for offset in range(1, hist_size):
        pl.semaphore_signal(
            barrier, 1, device_id={"hist": lax.rem(here + offset, hist_size)}, device_id_type=MESH
        )
    pl.semaphore_wait(barrier, mom_size + hist_size - 2)

    stat_row, stat_old = stat_now_ref[...], stat_prev_ref[...]
    spec_row, spec_old = spec_now_ref[...], spec_prev_ref[...]
    frequency = frequency_ref[pl.ds(pl.multiple_of(me * mode_count, mode_count), mode_count), :][
        :, 0:1
    ]
    lane = lax.broadcasted_iota(jnp.int32, (1, LANES), 1)
    first_half = lane < 2 * piece
    is_stat = (lane & (2 * piece - 1)) < piece
    sends = []

    for step in range(STEPS):
        edge = jnp.broadcast_to(
            jnp.sum(stat_row[:, time_count - 1 : time_count], axis=0, keepdims=True), (8, LANES)
        )
        for target in range(mom_size):
            span = slice(target * piece, (target + 1) * piece)
            row_send[step, target, 0:half, :] = jnp.concatenate(
                [
                    stat_row[:half, span],
                    spec_row[:half, span],
                    stat_row[half:, span],
                    spec_row[half:, span],
                ],
                axis=1,
            )
            row_send[step, target, half : half + 8, :] = edge
        row_copies = []
        for offset in range(1, mom_size):
            target = lax.rem(me + offset, mom_size)
            source = lax.rem(me + mom_size - offset, mom_size)
            out = copy_to(
                "mom",
                target,
                row_send.at[step, target],
                row_recv.at[step, me],
                row_sem.at[0, step, offset],
                row_sem.at[1, step, me],
            )
            out.start()
            sends.append(out)
            row_copies.append(
                copy_to(
                    "mom",
                    target,
                    row_send.at[step, source],
                    row_recv.at[step, source],
                    row_sem.at[0, step, offset],
                    row_sem.at[1, step, source],
                )
            )
        row_recv[step, me] = row_send[step, me]

        if step == 0:
            place = lax.broadcasted_iota(jnp.int32, (LANES, depth), 0)
            first = lax.broadcasted_iota(jnp.int32, (LANES, depth), 1)
            for kind in range(2):
                for part in range(2):
                    start = part * 2 * piece + (1 - kind) * piece
                    slot = (place - start) * mode_count
                    inside = (first >= slot) & (first < slot + mode_count)
                    spread[2 * kind + part] = jnp.where(
                        inside, 1.0 if kind == 0 else -1.0, 0.0
                    ).astype(jnp.bfloat16)

            late = lax.broadcasted_iota(jnp.int32, (depth, time_count), 1) * mode_count
            entry = lax.broadcasted_iota(jnp.int32, (depth, time_count), 0)

            def fill(block, carry):
                row = entry + block * depth
                span = pl.ds(pl.multiple_of(block * depth, depth), depth)
                low_mask[span, :] = jnp.where(row < late + mode_count, 1.0, 0.0).astype(
                    jnp.bfloat16
                )
                up_mask[span, :] = jnp.where(row >= late, 1.0, 0.0).astype(jnp.bfloat16)
                return carry

            lax.fori_loop(0, mom_size, fill, 0)

        for copy in row_copies:
            copy.wait_recv()
        edge_total = row_recv[step, 0, half : half + 8, :]
        for source in range(1, mom_size):
            edge_total = edge_total + row_recv[step, source, half : half + 8, :]
        edge_send[step] = edge_total
        edge_recv[step, here] = edge_total
        edge_copies = []
        for offset in range(1, hist_size):
            target = lax.rem(here + offset, hist_size)
            source = lax.rem(here + hist_size - offset, hist_size)
            out = copy_to(
                "hist",
                target,
                edge_send.at[step],
                edge_recv.at[step, here],
                edge_sem.at[0, step, offset],
                edge_sem.at[1, step, here],
            )
            out.start()
            sends.append(out)
            edge_copies.append(
                copy_to(
                    "hist",
                    target,
                    edge_send.at[step],
                    edge_recv.at[step, source],
                    edge_sem.at[0, step, offset],
                    edge_sem.at[1, step, source],
                )
            )

        rows = row_recv[step, :, 0:half, :].reshape(mom_size * half, LANES)
        both = jnp.dot(
            forward_ref[...], rows, precision=highest, preferred_element_type=jnp.float32
        )
        chosen = jnp.where(first_half, both[:mode_total], both[mode_total:])
        pos = chosen + pltpu.roll(chosen, 2 * piece, 1)
        swapped = pltpu.roll(pos, piece, 1)
        pos_stat = jnp.where(is_stat, pos, swapped)
        pos_spec = jnp.where(is_stat, swapped, pos)
        self_stat, self_spec = self_energy(pos_stat, pos_spec)
        both = jnp.dot(
            back_ref[...],
            jnp.where(is_stat, self_stat, self_spec),
            precision=highest,
            preferred_element_type=jnp.float32,
        )
        self_rows = jnp.where(first_half, both[: mom_size * half], both[mom_size * half :])
        self_send[step] = self_rows.astype(jnp.bfloat16).reshape(mom_size, half, LANES)
        self_copies = []
        for offset in range(1, mom_size):
            target = lax.rem(me + offset, mom_size)
            source = lax.rem(me + mom_size - offset, mom_size)
            out = copy_to(
                "mom",
                target,
                self_send.at[step, target],
                self_recv.at[step, me],
                self_sem.at[0, step, offset],
                self_sem.at[1, step, me],
            )
            out.start()
            sends.append(out)
            self_copies.append(
                copy_to(
                    "mom",
                    target,
                    self_send.at[step, source],
                    self_recv.at[step, source],
                    self_sem.at[0, step, offset],
                    self_sem.at[1, step, source],
                )
            )
        self_recv[step, me] = self_send[step, me]
        for copy in self_copies:
            copy.wait_recv()

        arrived = self_recv[step].reshape(mom_size * half, LANES)
        mode = lax.broadcasted_iota(jnp.int32, (mom_size * half, depth), 1) & (mode_count - 1)
        owner = lax.broadcasted_iota(jnp.int32, (mom_size * half, depth), 0) & (half - 1)
        for kind in range(2):
            for part in range(2):
                wide = jnp.dot(
                    arrived, spread[2 * kind + part], preferred_element_type=jnp.float32
                )
                wide = jnp.where(mode == owner + part * half, wide, 0.0).astype(jnp.bfloat16)
                begin = kind * mode_count + part * half
                weights[:, begin : begin + half, :] = wide.reshape(mom_size, half, depth)

        zeros = jnp.zeros((mode_count, time_count), jnp.float32)
        part_copies = []
        for turn in order:
            if step == 0:
                loads[turn, 0].wait()
                loads[turn, 1].wait()
            if turn:
                target = lax.rem(here + turn, hist_size)
                source = lax.rem(here + hist_size - turn, hist_size)
                wrapped = (here + turn) // hist_size
                select = pl.multiple_of((1 - wrapped) * mode_count, mode_count)

                def add(block, sums):
                    span = pl.ds(pl.multiple_of(block * depth, depth), depth)
                    return (
                        sums[0]
                        + jnp.dot(
                            weights[block, 0:mode_count, :],
                            stat_held[turn, span, :],
                            preferred_element_type=jnp.float32,
                        ),
                        sums[1]
                        + jnp.dot(
                            weights[block, pl.ds(select, mode_count), :],
                            spec_held[turn, span, :],
                            preferred_element_type=jnp.float32,
                        ),
                    )

                stat_sum, spec_sum = lax.fori_loop(0, mom_size, add, (zeros, zeros))
                below = wrapped.astype(jnp.float32)
                part_send[step, turn, 0:mode_count, :] = (
                    stat_sum + (1.0 - below) * spec_sum
                ).astype(jnp.bfloat16)
                part_send[step, turn, mode_count:, :] = (below * spec_sum).astype(jnp.bfloat16)
                out = copy_to(
                    "hist",
                    target,
                    part_send.at[step, turn],
                    part_recv.at[step, here],
                    part_sem.at[0, step, turn],
                    part_sem.at[1, step, here],
                )
                out.start()
                sends.append(out)
                part_copies.append(
                    (
                        source,
                        copy_to(
                            "hist",
                            target,
                            part_send.at[step, turn],
                            part_recv.at[step, source],
                            part_sem.at[0, step, turn],
                            part_sem.at[1, step, source],
                        ),
                    )
                )
            else:

                def add_own(block, sums):
                    span = pl.ds(pl.multiple_of(block * depth, depth), depth)
                    rho = spec_held[0, span, :]
                    own = weights[block, 0:mode_count, :]
                    return (
                        sums[0]
                        + jnp.dot(own, stat_held[0, span, :], preferred_element_type=jnp.float32)
                        + jnp.dot(
                            weights[block, mode_count:, :],
                            rho * low_mask[span, :],
                            preferred_element_type=jnp.float32,
                        ),
                        sums[1]
                        + jnp.dot(
                            own, rho * up_mask[span, :], preferred_element_type=jnp.float32
                        ),
                    )

                stat_sum, spec_sum = lax.fori_loop(0, mom_size, add_own, (zeros, zeros))

        for copy in edge_copies:
            copy.wait_recv()
        tadpole = (tadpole_coupling / mode_total) * edge_recv[step, hist_size - 1][0:1, 0:1]
        for source, copy in part_copies:
            copy.wait_recv()
            stat_sum = stat_sum + part_recv[step, source, 0:mode_count, :].astype(jnp.float32)
            spec_sum = spec_sum + part_recv[step, source, mode_count:, :].astype(jnp.float32)
        memory_stat = time_step * stat_sum
        memory_spec = time_step * spec_sum
        square = time_step * time_step
        stiffness = frequency + tadpole
        new_stat = 2.0 * stat_row - stat_old - square * (stiffness * stat_row + memory_stat)
        new_spec = 2.0 * spec_row - spec_old - square * (stiffness * spec_row + memory_spec)
        stat_old, stat_row = stat_row, new_stat
        spec_old, spec_row = spec_row, new_spec

    stat_end_ref[...] = stat_row
    spec_end_ref[...] = spec_row
    memory_stat_ref[...] = memory_stat
    memory_spec_ref[...] = memory_spec
    for out in sends:
        out.wait_send()


def sine_blocks(mode_total, mom_size):
    ordinal = np.arange(mode_total, dtype=np.float64) + 1.0
    sine = np.sqrt(2.0 / (mode_total + 1.0)) * np.sin(
        np.pi * ordinal[:, None] * ordinal[None, :] / (mode_total + 1.0)
    )
    split = sine.reshape(mode_total, mom_size, 2, -1)
    lower = split[:, :, 0, :].reshape(mode_total, -1)
    upper = split[:, :, 1, :].reshape(mode_total, -1)
    forward = np.concatenate([lower, upper], axis=0)
    back = np.concatenate([lower.T, upper.T], axis=0)
    frequency = bare_mass + 4.0 * np.sin(np.pi * ordinal / (2.0 * (mode_total + 1.0))) ** 2
    frequency = np.repeat(frequency[:, None], LANES, axis=1)
    return tuple(np.ascontiguousarray(a, np.float32) for a in (forward, back, frequency))


def per_device(
    statistic_now, statistic_prev, spectral_now, spectral_prev, statistic_hist, spectral_hist
):
    mode_count, time_count = statistic_now.shape
    hist_size = lax.axis_size("hist")
    mom_size = lax.axis_size("mom")
    window = statistic_hist.shape[2]
    piece = time_count // mom_size
    half = mode_count // 2
    fits = (
        4 * piece * mom_size == LANES * mom_size
        and half % ROWS == 0
        and mode_count & (mode_count - 1) == 0
        and time_count % LANES == 0
        and hist_size > 1
        and mom_size > 1
    )
    if not fits:
        return plain_device(
            statistic_now, statistic_prev, spectral_now, spectral_prev, statistic_hist, spectral_hist
        )
    mode_total = mode_count * mom_size
    total = time_count * mode_count
    depth = piece * mode_count
    constants = sine_blocks(mode_total, mom_size)
    vmem = pl.BlockSpec(memory_space=pltpu.VMEM)
    far = pl.BlockSpec(memory_space=pl.ANY)
    dma = pltpu.SemaphoreType.DMA
    return pl.pallas_call(
        functools.partial(fused_kernel, hist_size, mom_size),
        out_shape=(jax.ShapeDtypeStruct((mode_count, time_count), jnp.float32),) * 4,
        in_specs=[vmem] * 4 + [far] * 2 + [vmem] * 3,
        out_specs=(vmem,) * 4,
        scratch_shapes=[
            pltpu.VMEM((hist_size, total, time_count), jnp.bfloat16),
            pltpu.VMEM((hist_size, total, time_count), jnp.bfloat16),
            pltpu.VMEM((total, time_count), jnp.bfloat16),
            pltpu.VMEM((total, time_count), jnp.bfloat16),
            pltpu.VMEM((4, LANES, depth), jnp.bfloat16),
            pltpu.VMEM((mom_size, 2 * mode_count, depth), jnp.bfloat16),
            pltpu.VMEM((STEPS, mom_size, half + 8, LANES), jnp.float32),
            pltpu.VMEM((STEPS, mom_size, half + 8, LANES), jnp.float32),
            pltpu.VMEM((STEPS, mom_size, half, LANES), jnp.bfloat16),
            pltpu.VMEM((STEPS, mom_size, half, LANES), jnp.bfloat16),
            pltpu.VMEM((STEPS, hist_size, 2 * mode_count, time_count), jnp.bfloat16),
            pltpu.VMEM((STEPS, hist_size, 2 * mode_count, time_count), jnp.bfloat16),
            pltpu.VMEM((STEPS, 8, LANES), jnp.float32),
            pltpu.VMEM((STEPS, hist_size, 8, LANES), jnp.float32),
            dma((2, hist_size)),
            dma((2, STEPS, mom_size)),
            dma((2, STEPS, mom_size)),
            dma((2, STEPS, hist_size)),
            dma((2, STEPS, hist_size)),
        ],
        compiler_params=pltpu.CompilerParams(
            collective_id=0, has_side_effects=True, vmem_limit_bytes=56 * 1024 * 1024
        ),
        cost_estimate=pl.CostEstimate(
            flops=STEPS * 6 * total * window, bytes_accessed=4 * total * window, transcendentals=0
        ),
    )(
        statistic_now,
        statistic_prev,
        spectral_now,
        spectral_prev,
        statistic_hist.reshape(total, window),
        spectral_hist.reshape(total, window),
        *constants,
    )


def solution(mesh):
    placed = (
        P("mom", "hist"),
        P("mom", "hist"),
        P("mom", "hist"),
        P("mom", "hist"),
        P("hist", "mom", None),
        P("hist", "mom", None),
    )
    return jax.shard_map(
        per_device,
        mesh=mesh,
        in_specs=placed,
        out_specs=(P("mom", "hist"), P("mom", "hist"), P("mom", "hist"), P("mom", "hist")),
        check_vma=False,
    )
```

profile of v0, /device:TPU:0, one launch (start us, length us, event | category | flops | bytes accessed | tf_op | source)
XLA Modules:
  0.0 53.9 jit_solution(6159404804709733015)
XLA Ops:
  0.6 47.7 %shard_map.120 = (f32[32,256]{1,0:T(8,128)}, f32[32,256]{1,0:T(8,128)}, f32[32,256]{1,0:T(8,128)}, f32[32,256]{1,0:T(8,128)}) custom-call(f32[32,256]{1,0:T(8,128)} %stat_now_ref.1, f32[32,256]{1,0:T(8,128)} %stat_prev_ref.1, f32[32,256]{1,0:T(8,128)} %spec_now_ref.1, f32[32,256]{1,0:T(8,128)} %spec_prev_ref.1, bf16[8192,1024]{1,0:T(8,128)(2,1)} %bitcast.2, ...), custom_call_target="tpu_custom_call" | custom-call | flops 100663296 | bytes 33554432 | tf_op jit(solution)/shard_map/pallas_call | solution.py:522
  48.4 1.4 %copy.17 = f32[32,256]{1,0:T(8,128)} copy(f32[32,256]{1,0:T(8,128)} %get-tuple-element.8) | data formatting | bytes 65536
  49.8 1.4 %copy.18 = f32[32,256]{1,0:T(8,128)} copy(f32[32,256]{1,0:T(8,128)} %get-tuple-element.9) | data formatting | bytes 65536
  51.1 1.4 %copy.19 = f32[32,256]{1,0:T(8,128)} copy(f32[32,256]{1,0:T(8,128)} %get-tuple-element.10) | data formatting | bytes 65536
  52.5 1.4 %copy.20 = f32[32,256]{1,0:T(8,128)} copy(f32[32,256]{1,0:T(8,128)} %get-tuple-element.11) | data formatting | bytes 65536
where the time goes:
time: 54.3 us; the launch traced here: 53.9 us
  Pallas kernels  47.7 us (88%)
  local copies, waits for them, and re-layouts  5.5 us (10%)
  between operations  0.64 us (1%)
    pallas_call x1, Pallas kernels, per_device(): pl.pallas_call(functools.partial(fused_kernel, hist_size, mom_size), out_...  47.7 us
    unnamed x4, local copies, waits for them, and re-layouts  5.5 us

commit v1 on v0

--- a/solution.py
+++ b/solution.py
@@ -149,10 +149,7 @@
     forward_ref,
     back_ref,
     frequency_ref,
-    stat_end_ref,
-    spec_end_ref,
-    memory_stat_ref,
-    memory_spec_ref,
+    result_ref,
     stat_held,
     spec_held,
     low_mask,
@@ -172,6 +169,9 @@
     self_sem,
     part_sem,
     edge_sem,
+    mode_send,
+    mode_recv,
+    mode_sem,
 ):
     mode_count, time_count = stat_now_ref.shape
     half = mode_count // 2
@@ -181,6 +181,8 @@
     here = lax.axis_index("hist")
     me = lax.axis_index("mom")
     order = [*range(1, hist_size), 0]
+    rounds = 2 if mom_size % 2 == 0 else 1
+    round_depth = mom_size * depth // rounds
 
     loads = {}
     for turn in order:
@@ -202,7 +204,17 @@
         pl.semaphore_signal(
             barrier, 1, device_id={"hist": lax.rem(here + offset, hist_size)}, device_id_type=MESH
         )
-    pl.semaphore_wait(barrier, mom_size + hist_size - 2)
+
+    place = lax.broadcasted_iota(jnp.int32, (LANES, depth), 0)
+    first = lax.broadcasted_iota(jnp.int32, (LANES, depth), 1)
+    for kind in range(2):
+        for part in range(2):
+            start = part * 2 * piece + (1 - kind) * piece
+            slot = (place - start) * mode_count
+            inside = (first >= slot) & (first < slot + mode_count)
+            spread[2 * kind + part] = jnp.where(
+                inside, 1.0 if kind == 0 else -1.0, 0.0
+            ).astype(jnp.bfloat16)
 
     stat_row, stat_old = stat_now_ref[...], stat_prev_ref[...]
     spec_row, spec_old = spec_now_ref[...], spec_prev_ref[...]
@@ -220,7 +232,7 @@
         )
         for target in range(mom_size):
             span = slice(target * piece, (target + 1) * piece)
-            row_send[step, target, 0:half, :] = jnp.concatenate(
+            row_send[step, target] = jnp.concatenate(
                 [
                     stat_row[:half, span],
                     spec_row[:half, span],
@@ -229,7 +241,8 @@
                 ],
                 axis=1,
             )
-            row_send[step, target, half : half + 8, :] = edge
+        if step == 0:
+            pl.semaphore_wait(barrier, mom_size + hist_size - 2)
         row_copies = []
         for offset in range(1, mom_size):
             target = lax.rem(me + offset, mom_size)
@@ -255,19 +268,34 @@
                 )
             )
         row_recv[step, me] = row_send[step, me]
+        mode_send[step] = edge
+        mode_recv[step, me] = edge
+        mode_copies = []
+        for offset in range(1, mom_size):
+            target = lax.rem(me + offset, mom_size)
+            source = lax.rem(me + mom_size - offset, mom_size)
+            out = copy_to(
+                "mom",
+                target,
+                mode_send.at[step],
+                mode_recv.at[step, me],
+                mode_sem.at[0, step, offset],
+                mode_sem.at[1, step, me],
+            )
+            out.start()
+            sends.append(out)
+            mode_copies.append(
+                copy_to(
+                    "mom",
+                    target,
+                    mode_send.at[step],
+                    mode_recv.at[step, source],
+                    mode_sem.at[0, step, offset],
+                    mode_sem.at[1, step, source],
+                )
+            )
 
         if step == 0:
-            place = lax.broadcasted_iota(jnp.int32, (LANES, depth), 0)
-            first = lax.broadcasted_iota(jnp.int32, (LANES, depth), 1)
-            for kind in range(2):
-                for part in range(2):
-                    start = part * 2 * piece + (1 - kind) * piece
-                    slot = (place - start) * mode_count
-                    inside = (first >= slot) & (first < slot + mode_count)
-                    spread[2 * kind + part] = jnp.where(
-                        inside, 1.0 if kind == 0 else -1.0, 0.0
-                    ).astype(jnp.bfloat16)
-
             late = lax.broadcasted_iota(jnp.int32, (depth, time_count), 1) * mode_count
             entry = lax.broadcasted_iota(jnp.int32, (depth, time_count), 0)
 
@@ -284,9 +312,52 @@
 
         for copy in row_copies:
             copy.wait_recv()
-        edge_total = row_recv[step, 0, half : half + 8, :]
-        for source in range(1, mom_size):
-            edge_total = edge_total + row_recv[step, source, half : half + 8, :]
+        rows = row_recv[step].reshape(mom_size * half, LANES)
+        both = jnp.dot(
+            forward_ref[...], rows, precision=highest, preferred_element_type=jnp.float32
+        )
+        chosen = jnp.where(first_half, both[:mode_total], both[mode_total:])
+        pos = chosen + pltpu.roll(chosen, 2 * piece, 1)
+        swapped = pltpu.roll(pos, piece, 1)
+        pos_stat = jnp.where(is_stat, pos, swapped)
+        pos_spec = jnp.where(is_stat, swapped, pos)
+        self_stat, self_spec = self_energy(pos_stat, pos_spec)
+        both = jnp.dot(
+            back_ref[...],
+            jnp.where(is_stat, self_stat, self_spec),
+            precision=highest,
+            preferred_element_type=jnp.float32,
+        )
+        self_rows = jnp.where(first_half, both[: mom_size * half], both[mom_size * half :])
+        self_send[step] = self_rows.astype(jnp.bfloat16).reshape(mom_size, half, LANES)
+        self_copies = []
+        for offset in range(1, mom_size):
+            target = lax.rem(me + offset, mom_size)
+            source = lax.rem(me + mom_size - offset, mom_size)
+            out = copy_to(
+                "mom",
+                target,
+                self_send.at[step, target],
+                self_recv.at[step, me],
+                self_sem.at[0, step, offset],
+                self_sem.at[1, step, me],
+            )
+            out.start()
+            sends.append(out)
+            self_copies.append(
+                copy_to(
+                    "mom",
+                    target,
+                    self_send.at[step, source],
+                    self_recv.at[step, source],
+                    self_sem.at[0, step, offset],
+                    self_sem.at[1, step, source],
+                )
+            )
+        self_recv[step, me] = self_send[step, me]
+        for copy in mode_copies:
+            copy.wait_recv()
+        edge_total = jnp.sum(mode_recv[step], axis=0)
         edge_send[step] = edge_total
         edge_recv[step, here] = edge_total
         edge_copies = []
@@ -314,49 +385,6 @@
                 )
             )
 
-        rows = row_recv[step, :, 0:half, :].reshape(mom_size * half, LANES)
-        both = jnp.dot(
-            forward_ref[...], rows, precision=highest, preferred_element_type=jnp.float32
-        )
-        chosen = jnp.where(first_half, both[:mode_total], both[mode_total:])
-        pos = chosen + pltpu.roll(chosen, 2 * piece, 1)
-        swapped = pltpu.roll(pos, piece, 1)
-        pos_stat = jnp.where(is_stat, pos, swapped)
-        pos_spec = jnp.where(is_stat, swapped, pos)
-        self_stat, self_spec = self_energy(pos_stat, pos_spec)
-        both = jnp.dot(
-            back_ref[...],
-            jnp.where(is_stat, self_stat, self_spec),
-            precision=highest,
-            preferred_element_type=jnp.float32,
-        )
-        self_rows = jnp.where(first_half, both[: mom_size * half], both[mom_size * half :])
-        self_send[step] = self_rows.astype(jnp.bfloat16).reshape(mom_size, half, LANES)
-        self_copies = []
-        for offset in range(1, mom_size):
-            target = lax.rem(me + offset, mom_size)
-            source = lax.rem(me + mom_size - offset, mom_size)
-            out = copy_to(
-                "mom",
-                target,
-                self_send.at[step, target],
-                self_recv.at[step, me],
-                self_sem.at[0, step, offset],
-                self_sem.at[1, step, me],
-            )
-            out.start()
-            sends.append(out)
-            self_copies.append(
-                copy_to(
-                    "mom",
-                    target,
-                    self_send.at[step, source],
-                    self_recv.at[step, source],
-                    self_sem.at[0, step, offset],
-                    self_sem.at[1, step, source],
-                )
-            )
-        self_recv[step, me] = self_send[step, me]
         for copy in self_copies:
             copy.wait_recv()
 
@@ -370,7 +398,10 @@
                 )
                 wide = jnp.where(mode == owner + part * half, wide, 0.0).astype(jnp.bfloat16)
                 begin = kind * mode_count + part * half
-                weights[:, begin : begin + half, :] = wide.reshape(mom_size, half, depth)
+                for block in range(mom_size):
+                    weights[begin : begin + half, block * depth : (block + 1) * depth] = wide[
+                        block * half : (block + 1) * half
+                    ]
 
         zeros = jnp.zeros((mode_count, time_count), jnp.float32)
         part_copies = []
@@ -385,23 +416,23 @@
                 select = pl.multiple_of((1 - wrapped) * mode_count, mode_count)
 
                 def add(block, sums):
-                    span = pl.ds(pl.multiple_of(block * depth, depth), depth)
+                    span = pl.ds(pl.multiple_of(block * round_depth, round_depth), round_depth)
                     return (
                         sums[0]
                         + jnp.dot(
-                            weights[block, 0:mode_count, :],
+                            weights[0:mode_count, span],
                             stat_held[turn, span, :],
                             preferred_element_type=jnp.float32,
                         ),
                         sums[1]
                         + jnp.dot(
-                            weights[block, pl.ds(select, mode_count), :],
+                            weights[pl.ds(select, mode_count), span],
                             spec_held[turn, span, :],
                             preferred_element_type=jnp.float32,
                         ),
                     )
 
-                stat_sum, spec_sum = lax.fori_loop(0, mom_size, add, (zeros, zeros))
+                stat_sum, spec_sum = lax.fori_loop(0, rounds, add, (zeros, zeros))
                 below = wrapped.astype(jnp.float32)
                 part_send[step, turn, 0:mode_count, :] = (
                     stat_sum + (1.0 - below) * spec_sum
@@ -433,14 +464,14 @@
             else:
 
                 def add_own(block, sums):
-                    span = pl.ds(pl.multiple_of(block * depth, depth), depth)
+                    span = pl.ds(pl.multiple_of(block * round_depth, round_depth), round_depth)
                     rho = spec_held[0, span, :]
-                    own = weights[block, 0:mode_count, :]
+                    own = weights[0:mode_count, span]
                     return (
                         sums[0]
                         + jnp.dot(own, stat_held[0, span, :], preferred_element_type=jnp.float32)
                         + jnp.dot(
-                            weights[block, mode_count:, :],
+                            weights[mode_count:, span],
                             rho * low_mask[span, :],
                             preferred_element_type=jnp.float32,
                         ),
@@ -450,7 +481,7 @@
                         ),
                     )
 
-                stat_sum, spec_sum = lax.fori_loop(0, mom_size, add_own, (zeros, zeros))
+                stat_sum, spec_sum = lax.fori_loop(0, rounds, add_own, (zeros, zeros))
 
         for copy in edge_copies:
             copy.wait_recv()
@@ -468,12 +499,22 @@
         stat_old, stat_row = stat_row, new_stat
         spec_old, spec_row = spec_row, new_spec
 
-    stat_end_ref[...] = stat_row
-    spec_end_ref[...] = spec_row
-    memory_stat_ref[...] = memory_stat
-    memory_spec_ref[...] = memory_spec
+    for place, value in enumerate((stat_row, spec_row, memory_stat, memory_spec)):
+        result_ref[place] = value
     for out in sends:
         out.wait_send()
+
+
+def split_kernel(packed_ref, *refs):
+    *results, sem = refs
+    copies = [
+        pltpu.make_async_copy(packed_ref.at[place], result, sem.at[place])
+        for place, result in enumerate(results)
+    ]
+    for copy in copies:
+        copy.start()
+    for copy in copies:
+        copy.wait()
 
 
 def sine_blocks(mode_total, mom_size):
@@ -519,20 +560,20 @@
     vmem = pl.BlockSpec(memory_space=pltpu.VMEM)
     far = pl.BlockSpec(memory_space=pl.ANY)
     dma = pltpu.SemaphoreType.DMA
-    return pl.pallas_call(
+    packed = pl.pallas_call(
         functools.partial(fused_kernel, hist_size, mom_size),
-        out_shape=(jax.ShapeDtypeStruct((mode_count, time_count), jnp.float32),) * 4,
+        out_shape=jax.ShapeDtypeStruct((4, mode_count, time_count), jnp.float32),
         in_specs=[vmem] * 4 + [far] * 2 + [vmem] * 3,
-        out_specs=(vmem,) * 4,
+        out_specs=vmem,
         scratch_shapes=[
             pltpu.VMEM((hist_size, total, time_count), jnp.bfloat16),
             pltpu.VMEM((hist_size, total, time_count), jnp.bfloat16),
             pltpu.VMEM((total, time_count), jnp.bfloat16),
             pltpu.VMEM((total, time_count), jnp.bfloat16),
             pltpu.VMEM((4, LANES, depth), jnp.bfloat16),
-            pltpu.VMEM((mom_size, 2 * mode_count, depth), jnp.bfloat16),
-            pltpu.VMEM((STEPS, mom_size, half + 8, LANES), jnp.float32),
-            pltpu.VMEM((STEPS, mom_size, half + 8, LANES), jnp.float32),
+            pltpu.VMEM((2 * mode_count, total), jnp.bfloat16),
+            pltpu.VMEM((STEPS, mom_size, half, LANES), jnp.float32),
+            pltpu.VMEM((STEPS, mom_size, half, LANES), jnp.float32),
             pltpu.VMEM((STEPS, mom_size, half, LANES), jnp.bfloat16),
             pltpu.VMEM((STEPS, mom_size, half, LANES), jnp.bfloat16),
             pltpu.VMEM((STEPS, hist_size, 2 * mode_count, time_count), jnp.bfloat16),
@@ -544,6 +585,9 @@
             dma((2, STEPS, mom_size)),
             dma((2, STEPS, hist_size)),
             dma((2, STEPS, hist_size)),
+            pltpu.VMEM((STEPS, 8, LANES), jnp.float32),
+            pltpu.VMEM((STEPS, mom_size, 8, LANES), jnp.float32),
+            dma((2, STEPS, mom_size)),
         ],
         compiler_params=pltpu.CompilerParams(
             collective_id=0, has_side_effects=True, vmem_limit_bytes=56 * 1024 * 1024
@@ -560,6 +604,13 @@
         spectral_hist.reshape(total, window),
         *constants,
     )
+    return pl.pallas_call(
+        split_kernel,
+        out_shape=(jax.ShapeDtypeStruct((mode_count, time_count), jnp.float32),) * 4,
+        in_specs=[far],
+        out_specs=(far,) * 4,
+        scratch_shapes=[dma((4,))],
+    )(packed)
 
 
 def solution(mesh):

time: 54.3 us -> 49.4 us (0.910)
  local copies, waits for them, and re-layouts: 5.5 us -> 0 us
  Pallas kernels: 47.7 us -> 48.6 us
    unnamed x4 -> x0, local copies, waits for them, and re-layouts: 5.5 us -> none
    pallas_call x0 -> x1, Pallas kernels: none -> 5.11 us  [per_device(): pl.pallas_call(split_kernel, out_shape=(jax.ShapeDtypeStruct((mode_count,...]
    pallas_call x1, Pallas kernels: 47.7 us -> 43.5 us  [per_device(): pl.pallas_call(functools.partial(fused_kernel, hist_size, mom_size), out_...]
where the time goes in v1:
time: 49.4 us; the launch traced here: 49.3 us
  Pallas kernels  48.6 us (98%)
  between operations  0.64 us (1%)
    pallas_call x1, Pallas kernels, per_device(): pl.pallas_call(functools.partial(fused_kernel, hist_size, mom_size), out_...  43.5 us
    pallas_call x1, Pallas kernels, per_device(): pl.pallas_call(split_kernel, out_shape=(jax.ShapeDtypeStruct((mode_count,...  5.11 us

profile of v1, /device:TPU:0, one launch (start us, length us, event | category | flops | bytes accessed | tf_op | source)
XLA Modules:
  0.0 49.3 jit_solution(6574567284334089514)
XLA Ops:
  0.6 43.5 %shard_map.120.packed_ref = f32[4,32,256]{2,1,0:T(8,128)} custom-call(f32[32,256]{1,0:T(8,128)} %stat_now_ref.1, f32[32,256]{1,0:T(8,128)} %stat_prev_ref.1, f32[32,256]{1,0:T(8,128)} %spec_now_ref.1, f32[32,256]{1,0:T(8,128)} %spec_prev_ref.1, bf16[8192,1024]{1,0:T(8,128)(2,1)} %bitcast.2, bf16[8192,1024]{1,0:T(8,128)(2,1)} %bitcast.3, ...), custom_call_target="tpu_custom_call" | custom-call | flops 100663296 | bytes 33554432 | tf_op jit(solution)/shard_map/pallas_call | solution.py:563
  44.2 5.1 %shard_map.121 = (f32[32,256]{1,0:T(8,128)}, f32[32,256]{1,0:T(8,128)}, f32[32,256]{1,0:T(8,128)}, f32[32,256]{1,0:T(8,128)}) custom-call(f32[4,32,256]{2,1,0:T(8,128)} %shard_map.120.packed_ref), custom_call_target="tpu_custom_call" | custom-call | tf_op jit(solution)/shard_map/pallas_call | solution.py:607

commit v2 on v1

--- a/solution.py
+++ b/solution.py
@@ -172,6 +172,7 @@
     mode_send,
     mode_recv,
     mode_sem,
+    wide_spec,
 ):
     mode_count, time_count = stat_now_ref.shape
     half = mode_count // 2
@@ -181,8 +182,9 @@
     here = lax.axis_index("hist")
     me = lax.axis_index("mom")
     order = [*range(1, hist_size), 0]
-    rounds = 2 if mom_size % 2 == 0 else 1
+    rounds = 4 if mom_size % 4 == 0 else mom_size
     round_depth = mom_size * depth // rounds
+    round_times = time_count // rounds
 
     loads = {}
     for turn in order:
@@ -403,6 +405,28 @@
                         block * half : (block + 1) * half
                     ]
 
+        def widen(block, carry):
+            for part in range(2):
+                begin = (2 * part + 1) * piece
+                values = self_recv[step, block].astype(jnp.float32)
+                for late in range(piece):
+                    wide_spec[block * piece + late, part * half : (part + 1) * half, :] = (
+                        jnp.broadcast_to(
+                            values[:, begin + late : begin + late + 1], (half, LANES)
+                        )
+                    )
+            return carry
+
+        lax.fori_loop(0, mom_size, widen, 0)
+
+        def add_stat(turn, block, total):
+            for late in range(round_times):
+                when = block * round_times + late
+                span = pl.ds(pl.multiple_of(when * mode_count, mode_count), mode_count)
+                factor = jnp.concatenate([wide_spec[when]] * (time_count // LANES), axis=1)
+                total = total + factor * stat_held[turn, span, :].astype(jnp.float32)
+            return total
+
         zeros = jnp.zeros((mode_count, time_count), jnp.float32)
         part_copies = []
         for turn in order:
@@ -415,15 +439,10 @@
                 wrapped = (here + turn) // hist_size
                 select = pl.multiple_of((1 - wrapped) * mode_count, mode_count)
 
-                def add(block, sums):
+                def add(block, sums, turn=turn, select=select):
                     span = pl.ds(pl.multiple_of(block * round_depth, round_depth), round_depth)
                     return (
-                        sums[0]
-                        + jnp.dot(
-                            weights[0:mode_count, span],
-                            stat_held[turn, span, :],
-                            preferred_element_type=jnp.float32,
-                        ),
+                        add_stat(turn, block, sums[0]),
                         sums[1]
                         + jnp.dot(
                             weights[pl.ds(select, mode_count), span],
@@ -468,8 +487,7 @@
                     rho = spec_held[0, span, :]
                     own = weights[0:mode_count, span]
                     return (
-                        sums[0]
-                        + jnp.dot(own, stat_held[0, span, :], preferred_element_type=jnp.float32)
+                        add_stat(0, block, sums[0])
                         + jnp.dot(
                             weights[mode_count:, span],
                             rho * low_mask[span, :],
@@ -505,16 +523,9 @@
         out.wait_send()
 
 
-def split_kernel(packed_ref, *refs):
-    *results, sem = refs
-    copies = [
-        pltpu.make_async_copy(packed_ref.at[place], result, sem.at[place])
-        for place, result in enumerate(results)
-    ]
-    for copy in copies:
-        copy.start()
-    for copy in copies:
-        copy.wait()
+def split_kernel(packed_ref, *results):
+    for place, result in enumerate(results):
+        result[...] = packed_ref[place]
 
 
 def sine_blocks(mode_total, mom_size):
@@ -588,6 +599,7 @@
             pltpu.VMEM((STEPS, 8, LANES), jnp.float32),
             pltpu.VMEM((STEPS, mom_size, 8, LANES), jnp.float32),
             dma((2, STEPS, mom_size)),
+            pltpu.VMEM((time_count, mode_count, LANES), jnp.float32),
         ],
         compiler_params=pltpu.CompilerParams(
             collective_id=0, has_side_effects=True, vmem_limit_bytes=56 * 1024 * 1024
@@ -607,9 +619,8 @@
     return pl.pallas_call(
         split_kernel,
         out_shape=(jax.ShapeDtypeStruct((mode_count, time_count), jnp.float32),) * 4,
-        in_specs=[far],
-        out_specs=(far,) * 4,
-        scratch_shapes=[dma((4,))],
+        in_specs=[vmem],
+        out_specs=(vmem,) * 4,
     )(packed)
 
 

time: 49.4 us -> 49.9 us (1.010)
  Pallas kernels: 48.6 us -> 49.1 us
    pallas_call x1, Pallas kernels: 43.5 us -> 47.6 us  [per_device(): pl.pallas_call(functools.partial(fused_kernel, hist_size, mom_size), out_...]
    pallas_call x1, Pallas kernels: 5.11 us -> 1.56 us  [per_device(): pl.pallas_call(split_kernel, out_shape=(jax.ShapeDtypeStruct((mode_count,...]
where the time goes in v2:
time: 49.9 us; the launch traced here: 49.8 us
  Pallas kernels  49.1 us (98%)
  between operations  0.64 us (1%)
    pallas_call x1, Pallas kernels, per_device(): pl.pallas_call(functools.partial(fused_kernel, hist_size, mom_size), out_...  47.6 us
    pallas_call x1, Pallas kernels, per_device(): pl.pallas_call(split_kernel, out_shape=(jax.ShapeDtypeStruct((mode_count,...  1.56 us

profile of v2, /device:TPU:0, one launch (start us, length us, event | category | flops | bytes accessed | tf_op | source)
XLA Modules:
  0.0 49.8 jit_solution(7466392449982944661)
XLA Ops:
  0.6 47.6 %shard_map.120.packed_ref = f32[4,32,256]{2,1,0:T(8,128)} custom-call(f32[32,256]{1,0:T(8,128)} %stat_now_ref.1, f32[32,256]{1,0:T(8,128)} %stat_prev_ref.1, f32[32,256]{1,0:T(8,128)} %spec_now_ref.1, f32[32,256]{1,0:T(8,128)} %spec_prev_ref.1, bf16[8192,1024]{1,0:T(8,128)(2,1)} %bitcast.2, bf16[8192,1024]{1,0:T(8,128)(2,1)} %bitcast.3, ...), custom_call_target="tpu_custom_call" | custom-call | flops 100663296 | bytes 33554432 | tf_op jit(solution)/shard_map/pallas_call | solution.py:574
  48.2 1.6 %shard_map.121 = (f32[32,256]{1,0:T(8,128)}, f32[32,256]{1,0:T(8,128)}, f32[32,256]{1,0:T(8,128)}, f32[32,256]{1,0:T(8,128)}) custom-call(f32[4,32,256]{2,1,0:T(8,128)} %shard_map.120.packed_ref), custom_call_target="tpu_custom_call" | custom-call | tf_op jit(solution)/shard_map/pallas_call | solution.py:619

commit v3 on v1

--- a/solution.py
+++ b/solution.py
@@ -505,16 +505,9 @@
         out.wait_send()
 
 
-def split_kernel(packed_ref, *refs):
-    *results, sem = refs
-    copies = [
-        pltpu.make_async_copy(packed_ref.at[place], result, sem.at[place])
-        for place, result in enumerate(results)
-    ]
-    for copy in copies:
-        copy.start()
-    for copy in copies:
-        copy.wait()
+def split_kernel(packed_ref, *results):
+    for place, result in enumerate(results):
+        result[...] = packed_ref[place]
 
 
 def sine_blocks(mode_total, mom_size):
@@ -607,9 +600,8 @@
     return pl.pallas_call(
         split_kernel,
         out_shape=(jax.ShapeDtypeStruct((mode_count, time_count), jnp.float32),) * 4,
-        in_specs=[far],
-        out_specs=(far,) * 4,
-        scratch_shapes=[dma((4,))],
+        in_specs=[vmem],
+        out_specs=(vmem,) * 4,
     )(packed)
 
 

time: 49.4 us -> 45.9 us (0.929)
  Pallas kernels: 48.6 us -> 45.1 us
    pallas_call x1, Pallas kernels: 5.11 us -> 1.56 us  [per_device(): pl.pallas_call(split_kernel, out_shape=(jax.ShapeDtypeStruct((mode_count,...]
where the time goes in v3:
time: 45.9 us; the launch traced here: 45.7 us
  Pallas kernels  45.1 us (98%)
  between operations  0.64 us (1%)
    pallas_call x1, Pallas kernels, per_device(): pl.pallas_call(functools.partial(fused_kernel, hist_size, mom_size), out_...  43.5 us
    pallas_call x1, Pallas kernels, per_device(): pl.pallas_call(split_kernel, out_shape=(jax.ShapeDtypeStruct((mode_count,...  1.56 us

profile of v3, /device:TPU:0, one launch (start us, length us, event | category | flops | bytes accessed | tf_op | source)
XLA Modules:
  0.0 45.7 jit_solution(10465843037813191792)
XLA Ops:
  0.6 43.5 %shard_map.120.packed_ref = f32[4,32,256]{2,1,0:T(8,128)} custom-call(f32[32,256]{1,0:T(8,128)} %stat_now_ref.1, f32[32,256]{1,0:T(8,128)} %stat_prev_ref.1, f32[32,256]{1,0:T(8,128)} %spec_now_ref.1, f32[32,256]{1,0:T(8,128)} %spec_prev_ref.1, bf16[8192,1024]{1,0:T(8,128)(2,1)} %bitcast.2, bf16[8192,1024]{1,0:T(8,128)(2,1)} %bitcast.3, ...), custom_call_target="tpu_custom_call" | custom-call | flops 100663296 | bytes 33554432 | tf_op jit(solution)/shard_map/pallas_call | solution.py:556
  44.2 1.6 %shard_map.121 = (f32[32,256]{1,0:T(8,128)}, f32[32,256]{1,0:T(8,128)}, f32[32,256]{1,0:T(8,128)}, f32[32,256]{1,0:T(8,128)}) custom-call(f32[4,32,256]{2,1,0:T(8,128)} %shard_map.120.packed_ref), custom_call_target="tpu_custom_call" | custom-call | tf_op jit(solution)/shard_map/pallas_call | solution.py:600

commit v4 on v3

--- a/solution.py
+++ b/solution.py
@@ -146,9 +146,9 @@
     spec_prev_ref,
     stat_hist_ref,
     spec_hist_ref,
-    forward_ref,
-    back_ref,
-    frequency_ref,
+    forward_far,
+    back_far,
+    frequency_far,
     result_ref,
     stat_held,
     spec_held,
@@ -172,6 +172,10 @@
     mode_send,
     mode_recv,
     mode_sem,
+    forward_ref,
+    back_ref,
+    frequency_ref,
+    table_sem,
 ):
     mode_count, time_count = stat_now_ref.shape
     half = mode_count // 2
@@ -181,8 +185,21 @@
     here = lax.axis_index("hist")
     me = lax.axis_index("mom")
     order = [*range(1, hist_size), 0]
-    rounds = 2 if mom_size % 2 == 0 else 1
+    rounds = 1
     round_depth = mom_size * depth // rounds
+
+    tables = [
+        pltpu.make_async_copy(whole, held, table_sem.at[place])
+        for place, (whole, held) in enumerate(
+            (
+                (forward_far, forward_ref),
+                (back_far, back_ref),
+                (frequency_far, frequency_ref),
+            )
+        )
+    ]
+    for table in tables:
+        table.start()
 
     loads = {}
     for turn in order:
@@ -218,9 +235,6 @@
 
     stat_row, stat_old = stat_now_ref[...], stat_prev_ref[...]
     spec_row, spec_old = spec_now_ref[...], spec_prev_ref[...]
-    frequency = frequency_ref[pl.ds(pl.multiple_of(me * mode_count, mode_count), mode_count), :][
-        :, 0:1
-    ]
     lane = lax.broadcasted_iota(jnp.int32, (1, LANES), 1)
     first_half = lane < 2 * piece
     is_stat = (lane & (2 * piece - 1)) < piece
@@ -312,6 +326,12 @@
 
         for copy in row_copies:
             copy.wait_recv()
+        if step == 0:
+            for table in tables:
+                table.wait()
+            frequency = frequency_ref[pl.ds(pl.multiple_of(me * mode_count, mode_count), mode_count), :][
+                :, 0:1
+            ]
         rows = row_recv[step].reshape(mom_size * half, LANES)
         both = jnp.dot(
             forward_ref[...], rows, precision=highest, preferred_element_type=jnp.float32
@@ -556,7 +576,7 @@
     packed = pl.pallas_call(
         functools.partial(fused_kernel, hist_size, mom_size),
         out_shape=jax.ShapeDtypeStruct((4, mode_count, time_count), jnp.float32),
-        in_specs=[vmem] * 4 + [far] * 2 + [vmem] * 3,
+        in_specs=[vmem] * 4 + [far] * 5,
         out_specs=vmem,
         scratch_shapes=[
             pltpu.VMEM((hist_size, total, time_count), jnp.bfloat16),
@@ -581,6 +601,8 @@
             pltpu.VMEM((STEPS, 8, LANES), jnp.float32),
             pltpu.VMEM((STEPS, mom_size, 8, LANES), jnp.float32),
             dma((2, STEPS, mom_size)),
+            *[pltpu.VMEM(table.shape, jnp.float32) for table in constants],
+            dma((3,)),
         ],
         compiler_params=pltpu.CompilerParams(
             collective_id=0, has_side_effects=True, vmem_limit_bytes=56 * 1024 * 1024

time: 45.9 us -> 48.7 us (1.061)
  Pallas kernels: 45.1 us -> 47.9 us
    pallas_call x1, Pallas kernels: 43.5 us -> 46.3 us  [per_device(): pl.pallas_call(functools.partial(fused_kernel, hist_size, mom_size), out_...]
where the time goes in v4:
time: 48.7 us; the launch traced here: 48.5 us
  Pallas kernels  47.9 us (98%)
  between operations  0.64 us (1%)
    pallas_call x1, Pallas kernels, per_device(): pl.pallas_call(functools.partial(fused_kernel, hist_size, mom_size), out_...  46.3 us
    pallas_call x1, Pallas kernels, per_device(): pl.pallas_call(split_kernel, out_shape=(jax.ShapeDtypeStruct((mode_count,...  1.56 us

profile of v4, /device:TPU:0, one launch (start us, length us, event | category | flops | bytes accessed | tf_op | source)
XLA Modules:
  0.0 48.5 jit_solution(8971995115549795954)
XLA Ops:
  0.6 46.3 %shard_map.120.packed_ref = f32[4,32,256]{2,1,0:T(8,128)} custom-call(f32[32,256]{1,0:T(8,128)} %stat_now_ref.1, f32[32,256]{1,0:T(8,128)} %stat_prev_ref.1, f32[32,256]{1,0:T(8,128)} %spec_now_ref.1, f32[32,256]{1,0:T(8,128)} %spec_prev_ref.1, bf16[8192,1024]{1,0:T(8,128)(2,1)} %bitcast.2, bf16[8192,1024]{1,0:T(8,128)(2,1)} %bitcast.3, ...), custom_call_target="tpu_custom_call" | custom-call | flops 100663296 | bytes 33554432 | tf_op jit(solution)/shard_map/pallas_call | solution.py:576
  47.0 1.6 %shard_map.121 = (f32[32,256]{1,0:T(8,128)}, f32[32,256]{1,0:T(8,128)}, f32[32,256]{1,0:T(8,128)}, f32[32,256]{1,0:T(8,128)}) custom-call(f32[4,32,256]{2,1,0:T(8,128)} %shard_map.120.packed_ref), custom_call_target="tpu_custom_call" | custom-call | tf_op jit(solution)/shard_map/pallas_call | solution.py:622
